TPU v7x, 32 devices: a whole 2x2x4 slice. The times are simulated.
32 devices in a mesh: scen: 4 (over z), net: 8 (over y, x, core).
Axes of the slice: x: 2, y: 2, z: 4, core: 2. Of those that a mesh axis runs over, the one named last changes fastest.
Arguments:
- coupling: bfloat16 [768, 64, 320], P('net'), may hold values from -0.3125 to 0.3125
- tie_blocks: bfloat16 [1024, 64, 128], P('net'), may hold values from -0.5 to 0.5
- w_pattern: int32 [768, 4], P('net'), may hold values from 0 to 127
- link_pattern: int32 [768], P('net'), may hold values from 0 to 127
- left_bounds: int32 [1024], P('net'), may hold values from 0 to 127
- right_bounds: int32 [1024], P('net'), may hold values from 0 to 127
- block_counts: int32 [8], P('net'), may hold values from 48 to 96, as said below
- commit_cost: float32 [1024, 64], P('net'), may hold values from -3 to 3
- dispatch_cost: float32 [1024, 64], P('net'), may hold values from -6 to 6
- demand: float32 [768, 64], P('net'), may hold values from -6 to 6
- wind_error: bfloat16 [768, 64, 512], P('net', None, 'scen'), may hold values from -3 to 3
- commit_start: float32 [1024, 64], P('net'), may hold values from 0 to 1
- dispatch_start: float32 [1024, 64, 512], P('net', None, 'scen'), may hold values from 0 to 2
- dual_start: float32 [768, 64, 512], P('net', None, 'scen'), may hold values from -8 to 8
- tie_start: float32 [1024, 64, 512], P('net', None, 'scen'), may hold values from -6 to 6
Outputs:
- commit_out: float32 [1024, 64], P('net')
- dispatch_out: float32 [1024, 64, 512], P('net', None, 'scen')
- dual_out: float32 [768, 64, 512], P('net', None, 'scen')
- tie_out: float32 [1024, 64, 512], P('net', None, 'scen')
Inputs may be any that keep to these rules, and one draw needn't show every extreme that they name: `block_counts`: some partition has all 96 row blocks active.
All inputs are finite; a program needn't handle non-finite values.
Results may differ from a plain program's by a relative error of at most 0.0035.
Values may be sent and summed in bfloat16 or wider, within the bound.
A program may use at most 192 MiB of HBM per device.

v0:
```python
import jax
import jax.numpy as jnp
from jax import lax
from jax.sharding import PartitionSpec as P

BLK = 64
KW = 4
ITERS = 2
YB = 128
XB = 128
primal_step = 0.4
first_step = 1.0
dual_step = 0.4


def from_behind(value, axis, by):
    devices = lax.axis_size(axis)
    pairs = [(i, i + by) for i in range(devices) if 0 <= i + by < devices]
    return lax.ppermute(value, axis, pairs)


def apply_blocks(block_mats, stacked):
    return jnp.einsum("roj,rjs->ros", block_mats, stacked, preferred_element_type=jnp.float32)


def transpose_blocks(block_mats, dual_rows):
    return jnp.einsum("roj,ros->rjs", block_mats, dual_rows, preferred_element_type=jnp.float32)


def one_hot_rows(indices, count):
    return (indices[None, :] == jnp.arange(count, dtype=jnp.int32)[:, None]).astype(jnp.float32)


def sum_into(selector, terms):
    return jnp.einsum(
        "bk,kos->bos",
        selector,
        terms,
        precision=lax.Precision.HIGHEST,
        preferred_element_type=jnp.float32,
    )


def body(
    coupling,
    tie_blocks,
    w_pattern,
    link_pattern,
    left_bounds,
    right_bounds,
    block_counts,
    commit_cost,
    dispatch_cost,
    demand,
    wind_error,
    commit_start,
    dispatch_start,
    dual_start,
    tie_start,
):
    row_count = coupling.shape[0]
    scen_dev = dispatch_start.shape[2]
    scen_total = scen_dev * lax.axis_size("scen")
    lead = KW * BLK
    live_tie = (lax.axis_index("net") < lax.axis_size("net") - 1).astype(jnp.float32)
    active = (jnp.arange(row_count) < block_counts[0]).astype(jnp.float32)[:, None, None]
    pattern_select = one_hot_rows(w_pattern.reshape(-1), YB)
    link_select = one_hot_rows(link_pattern, XB)
    right_select = one_hot_rows(right_bounds, YB)
    left_select = one_hot_rows(left_bounds, YB)
    recourse = coupling[:, :, :lead]
    linking = coupling[:, :, lead:]
    cost_col = dispatch_cost[:, :, None]
    target = demand[:, :, None] + wind_error.astype(jnp.float32)
    first_now = commit_start
    second_now = dispatch_start
    dual_now = dual_start * active
    tie_now = tie_start * live_tie
    for iteration in range(ITERS):
        dual_half = dual_now.astype(jnp.bfloat16)
        tie_half = tie_now.astype(jnp.bfloat16)
        recourse_terms = transpose_blocks(recourse, dual_half).reshape(
            row_count * KW, BLK, scen_dev
        )
        grad_second = sum_into(pattern_select, recourse_terms)
        link_terms = (
            jnp.einsum("roj,ros->rj", linking, dual_half, preferred_element_type=jnp.float32)
            / scen_total
        )
        grad_part = jnp.dot(
            link_select,
            link_terms,
            precision=lax.Precision.HIGHEST,
            preferred_element_type=jnp.float32,
        )
        tie_terms = transpose_blocks(tie_blocks, tie_half)
        own_terms = tie_terms[:, :BLK]
        left_terms = from_behind(tie_terms[:, BLK:], "net", 1)
        grad_second = grad_second + sum_into(right_select, own_terms)
        grad_second = grad_second + sum_into(left_select, left_terms)
        grad_first = lax.psum(grad_part.astype(jnp.bfloat16), "scen").astype(jnp.float32)
        first_next = jnp.clip(first_now - first_step * (commit_cost - grad_first), 0.0, 1.0)
        second_next = jnp.maximum(second_now - primal_step * (cost_col - grad_second), 0.0)
        first_bar = (2.0 * first_next - first_now).astype(jnp.bfloat16)
        second_bar = (2.0 * second_next - second_now).astype(jnp.bfloat16)
        next_rows = from_behind(second_bar[left_bounds], "net", -1)
        tie_inputs = jnp.concatenate([second_bar[right_bounds], next_rows], axis=1)
        tie_rows = apply_blocks(tie_blocks, tie_inputs)
        gathered = second_bar[w_pattern].reshape(row_count, lead, scen_dev)
        linked = jnp.einsum(
            "roi,ri->ro", linking, first_bar[link_pattern], preferred_element_type=jnp.float32
        )
        coupled = apply_blocks(recourse, gathered) + linked[:, :, None]
        dual_now = (dual_now + dual_step * (target - coupled)) * active
        tie_now = (tie_now - dual_step * tie_rows) * live_tie
        first_now = first_next
        second_now = second_next
    return (first_now, second_now, dual_now, tie_now)


def solution(mesh):
    return jax.shard_map(
        body,
        mesh=mesh,
        in_specs=(
            P("net", None, None),
            P("net", None, None),
            P("net", None),
            P("net"),
            P("net"),
            P("net"),
            P("net"),
            P("net", None),
            P("net", None),
            P("net", None),
            P("net", None, "scen"),
            P("net", None),
            P("net", None, "scen"),
            P("net", None, "scen"),
            P("net", None, "scen"),
        ),
        out_specs=(
            P("net", None),
            P("net", None, "scen"),
            P("net", None, "scen"),
            P("net", None, "scen"),
        ),
        check_vma=False,
    )
```

profile of v0, /device:TPU:0, one launch (start us, length us, event | category | flops | bytes accessed | tf_op | source)
XLA Modules:
  0.0 271.5 jit_solution(8567158418583271729)
XLA Ops:
  2.2 3.7 %convolution_bitcast_fusion.3 = f32[128,128,128]{2,1,0:T(8,128)S(1)} fusion(bf16[128,64,128]{2,1,0:T(8,128)(2,1)S(1)} %copy-done, f32[128,64,128]{2,1,0:T(8,128)} %param.29, f32[]{:T(128)S(6)} %convert_element_type.65), kind=kOutput, calls=%fused_computation.40 | convolution fusion | flops 270532608 | bytes 14680068 | tf_op jit(solution)/shard_map/roj,ros->rjs/dot_general | solution.py:27
  5.9 4.3 %fusion.85 = (f32[128,64,128]{2,1,0:T(8,128)}, f32[128,64,128]{2,1,0:T(8,128)}) fusion(f32[128,128,128]{2,1,0:T(8,128)S(1)} %convolution_bitcast_fusion.3), kind=kLoop, calls=%fused_computation.111 | loop fusion | bytes 16777216 | tf_op jit(solution)/shard_map/slice | solution.py:98
  10.2 4.3 %collective-permute-start = (f32[128,64,128]{2,1,0:T(8,128)}, f32[128,64,128]{2,1,0:T(8,128)}, u32[]{:S(2)}, u32[]{:S(2)}) collective-permute-start(f32[128,64,128]{2,1,0:T(8,128)} %get-tuple-element.16), channel_id=1, source_target_pairs={{0,1},{1,2},{2,3},{3,4},{4,5},{5,6},{6,7},{8,9},{9,10},{10,11},{11... | collective-permute-start | bytes 12582920 | tf_op jit(solution)/shard_map/ppermute | solution.py:19
  15.2 6.9 %convolution_bitcast_fusion.1 = f32[96,256,128]{1,2,0:T(8,128)} fusion(bf16[96,64,320]{2,1,0:T(8,128)(2,1)S(1)} %bitcast.81, f32[96,64,128]{2,1,0:T(8,128)S(1)} %copy-done.5, f32[96]{0:T(128)S(1)} %compare_convert_fusion), kind=kOutput, calls=%fused_computation.13 | convolution fusion | flops 404226048 | bytes 18874880 | tf_op jit(solution)/shard_map/roj,ros->rjs/dot_general | solution.py:27
  22.1 12.8 %copy.33 = f32[96,256,128]{2,1,0:T(8,128)} copy(f32[96,256,128]{1,2,0:T(8,128)} %convolution_bitcast_fusion.1) | data formatting | bytes 25165824 | tf_op jit(solution)/shard_map/roj,ros->rjs/dot_general | solution.py:27
  35.2 6.7 %fusion.20 = f32[128,64,128]{2,0,1:T(8,128)S(1)} fusion(f32[128,64,128]{2,1,0:T(8,128)} %get-tuple-element.17, s32[128]{0:T(128)S(1)} %copy-done.16), kind=kOutput, calls=%fused_computation.32 | convolution fusion | flops 1610629120 | bytes 8389120 | tf_op jit(solution)/shard_map/bk,kos->bos/dot_general | solution.py:35
  41.9 16.6 %fusion.2 = f32[128,64,128]{2,0,1:T(8,128)S(1)} fusion(f32[384,64,128]{2,1,0:T(8,128)} %bitcast.78, s32[384]{0:T(512)S(1)} %eq.57), kind=kOutput, calls=%fused_computation.10 | convolution fusion | flops 4831887360 | bytes 16778752 | tf_op jit(solution)/shard_map/bk,kos->bos/dot_general | solution.py:35
  58.6 13.5 %subtract_convert_fusion.1 = (bf16[128,64,128]{2,0,1:T(8,128)(2,1)S(1)}, f32[128,64,128]{2,0,1:T(8,128)}) fusion(f32[128,64,128]{2,1,0:T(8,128)S(1)} %copy-done.9, f32[128,64,128]{2,1,0:T(8,128)} %collective-permute-done, s32[128]{0:T(128)S(1)} %copy-done.15, f32[128,64,128]{2,0,1:T(8,128)S(1)} %fusion.2, f32[128,64,128]{2,0,1:T(8,128)S(1)} %fusion.20, ...), kind=kOutput, calls=%fused_computation.36 | convolution fusion | flops 1620066304 | bytes 23101952 | tf_op jit(solution)/shard_map/bk,kos->bos/dot_general | solution.py:35
  72.1 2.7 copy.40
  74.7 3.7 %gather_fusion.3 = bf16[128,64,128]{2,1,0:T(8,128)(2,1)} fusion(bf16[128,64,128]{2,1,0:T(8,128)(2,1)} %copy.40, s32[1024]{0:T(1024)S(1)} %pad_clamp_fusion), kind=kCustom, calls=%fused_computation.3 | custom fusion | bytes 4194816 | tf_op jit(solution)/shard_map/gather | solution.py:106
  79.8 2.9 %convert_reduce_fusion.1 = f32[96,64]{1,0:T(8,128)S(1)} fusion(f32[96,64,128]{2,1,0:T(8,128)} %param.28, f32[96]{0:T(128)S(1)} %compare_convert_fusion), kind=kLoop, calls=%fused_computation.51 | loop fusion | flops 3139584 | bytes 3170688 | tf_op jit(solution)/shard_map/roj,ros->rj/reduce_sum | solution.py:87
  82.7 3.7 %gather_fusion.2 = bf16[128,64,128]{2,1,0:T(8,128)(2,1)} fusion(bf16[128,64,128]{2,1,0:T(8,128)(2,1)} %copy.40, s32[1024]{0:T(1024)S(1)} %pad_clamp_fusion.1), kind=kCustom, calls=%fused_computation.2 | custom fusion | bytes 4194816 | tf_op jit(solution)/shard_map/gather | solution.py:107
  86.7 4.7 %fusion.13 = f32[128,64,128]{2,1,0:T(8,128)S(1)} fusion(f32[128,64,128]{2,1,0:T(8,128)} %param.29, bf16[128,64,128]{2,1,0:T(8,128)(2,1)S(1)} %copy-done, bf16[128,64,128]{2,1,0:T(8,128)(2,1)} %collective-permute-done.1, bf16[128,64,128]{2,1,0:T(8,128)(2,1)} %gather_fusion.2, f32[]{:T(128)S(6)} %convert_element_type.65), kind=kOutput, calls=%fused_computation.25 | convolution fusion | flops 281018368 | bytes 14680068 | tf_op jit(solution)/shard_map/roj,rjs->ros/dot_general | solution.py:23
  94.7 4.2 %fusion.84 = (f32[128,64,128]{2,1,0:T(8,128)}, f32[128,64,128]{2,1,0:T(8,128)}) fusion(f32[128,128,128]{2,1,0:T(8,128)S(1)} %convolution_bitcast_fusion.2), kind=kLoop, calls=%fused_computation.110 | loop fusion | bytes 16777216 | tf_op jit(solution)/shard_map/slice | solution.py:98
  98.9 26.5 %collective-permute-start.2 = (f32[128,64,128]{2,1,0:T(8,128)}, f32[128,64,128]{2,1,0:T(8,128)}, u32[]{:S(2)}, u32[]{:S(2)}) collective-permute-start(f32[128,64,128]{2,1,0:T(8,128)} %get-tuple-element.14), channel_id=1, source_target_pairs={{0,1},{1,2},{2,3},{3,4},{4,5},{5,6},{6,7},{8,9},{9,10},{10,11},{11... | collective-permute-start | bytes 12582920 | tf_op jit(solution)/shard_map/ppermute | solution.py:19
  127.6 19.2 %psum.14 = bf16[128,64]{0,1:T(8,128)(2,1)S(1)} all-reduce(bf16[128,64]{0,1:T(8,128)(2,1)S(1)} %convolution_convert_fusion.1), channel_id=1, replica_groups=mesh['scen'=4,'net'=8] {'scen'}, use_global_device_ids=true, to_apply=%region_1.0 | all-reduce | flops 8192 | bytes 32768 | tf_op jit(solution)/shard_map/psum | solution.py:101
  148.0 2.3 fusion.52
  150.4 5.7 %gather_fusion = bf16[384,64,128]{2,1,0:T(8,128)(2,1)} fusion(bf16[128,64,128]{2,1,0:T(8,128)(2,1)} %copy.40, s32[1024]{0:T(1024)S(1)} %pad_clamp_fusion.3), kind=kCustom, calls=%fused_computation | custom fusion | bytes 12584448 | tf_op jit(solution)/shard_map/gather | solution.py:109
  156.0 6.8 %convert_reduce_fusion = (f32[96,64]{1,0:T(8,128)S(1)}, f32[96,64,128]{2,1,0:T(8,128)S(1)}) fusion(f32[96,64]{1,0:T(8,128)S(1)} %bitcast.93, bf16[96,256,128]{2,1,0:T(8,128)(2,1)} %bitcast.87, bf16[96,64,320]{2,1,0:T(8,128)(2,1)} %param.15, bf16[96,64,128]{2,1,0:T(8,128)(2,1)} %param.25, f32[96,64]{1,0:T(8,128)S(1)} %copy.31, f32[96,64,128]{2,1,0:T(8,128)} %param.28, ...), kind=kOutput, calls=%fused_computation.49 | convolution fusion | flops 411297792 | bytes 17375616 | tf_op jit(solution)/shard_map/roj,rjs->ros/dot_general | solution.py:23
  164.5 6.4 %convolution_bitcast_fusion = f32[96,256,128]{1,2,0:T(8,128)} fusion(bf16[96,64,320]{2,1,0:T(8,128)(2,1)S(1)} %bitcast.83, f32[96,64,128]{2,1,0:T(8,128)S(1)} %get-tuple-element.21), kind=kOutput, calls=%fused_computation.12 | convolution fusion | flops 403439616 | bytes 18874368 | tf_op jit(solution)/shard_map/roj,ros->rjs/dot_general | solution.py:27
  170.9 12.6 %copy.42 = f32[96,256,128]{2,1,0:T(8,128)} copy(f32[96,256,128]{1,2,0:T(8,128)} %convolution_bitcast_fusion) | data formatting | bytes 25165824 | tf_op jit(solution)/shard_map/roj,ros->rjs/dot_general | solution.py:27
  183.5 16.6 %fusion = f32[128,64,128]{2,0,1:T(8,128)S(1)} fusion(f32[384,64,128]{2,1,0:T(8,128)} %bitcast.79, s32[384]{0:T(512)S(1)} %eq.57), kind=kOutput, calls=%fused_computation.8 | convolution fusion | flops 4831887360 | bytes 16778752 | tf_op jit(solution)/shard_map/bk,kos->bos/dot_general | solution.py:35
  200.1 4.7 %fusion.16 = f32[128,64,128]{2,0,1:T(8,128)S(1)} fusion(f32[128,64,128]{2,1,0:T(8,128)S(1)} %copy-done.7, s32[128]{0:T(128)S(1)} %copy-done.16), kind=kOutput, calls=%fused_computation.28 | convolution fusion | flops 1610629120 | bytes 8389120 | tf_op jit(solution)/shard_map/bk,kos->bos/dot_general | solution.py:35
  204.8 9.8 %subtract_convert_fusion = (bf16[128,64,128]{2,0,1:T(8,128)(2,1)S(1)}, f32[128,64,128]{2,0,1:T(8,128)}) fusion(f32[128,64,128]{2,0,1:T(8,128)S(1)} %copy-done.6, f32[128,64,128]{2,1,0:T(8,128)} %collective-permute-done.2, s32[128]{0:T(128)S(1)} %copy-done.15, f32[128,64,128]{2,0,1:T(8,128)S(1)} %fusion, f32[128,64,128]{2,0,1:T(8,128)S(1)} %fusion.16, ...), kind=kOutput, calls=%fused_computation.34 | convolution fusion | flops 1620066304 | bytes 23101952 | tf_op jit(solution)/shard_map/bk,kos->bos/dot_general | solution.py:35
  214.6 2.7 copy.48
  217.3 3.8 %gather_fusion.7 = bf16[128,64,128]{2,1,0:T(8,128)(2,1)} fusion(bf16[128,64,128]{2,1,0:T(8,128)(2,1)} %copy.48, s32[1024]{0:T(1024)S(1)} %pad_clamp_fusion), kind=kCustom, calls=%fused_computation.7 | custom fusion | bytes 4194816 | tf_op jit(solution)/shard_map/gather | solution.py:106
  224.6 15.5 %psum.15 = bf16[128,64]{0,1:T(8,128)(2,1)S(1)} all-reduce(bf16[128,64]{0,1:T(8,128)(2,1)S(1)} %convolution_convert_fusion), channel_id=1, replica_groups=mesh['scen'=4,'net'=8] {'scen'}, use_global_device_ids=true, to_apply=%region_3.4 | all-reduce | flops 8192 | bytes 32768 | tf_op jit(solution)/shard_map/psum | solution.py:101
  243.8 5.6 %gather_fusion.4 = bf16[384,64,128]{2,1,0:T(8,128)(2,1)} fusion(bf16[128,64,128]{2,1,0:T(8,128)(2,1)} %copy.48, s32[1024]{0:T(1024)S(1)} %pad_clamp_fusion.3), kind=kCustom, calls=%fused_computation.4 | custom fusion | bytes 12584448 | tf_op jit(solution)/shard_map/gather | solution.py:109
  249.5 3.8 %gather_fusion.6 = bf16[128,64,128]{2,1,0:T(8,128)(2,1)} fusion(bf16[128,64,128]{2,1,0:T(8,128)(2,1)} %copy.48, s32[1024]{0:T(1024)S(1)} %pad_clamp_fusion.1), kind=kCustom, calls=%fused_computation.6 | custom fusion | bytes 4194816 | tf_op jit(solution)/shard_map/gather | solution.py:107
  253.3 6.8 %copy.52 = f32[128,64,128]{2,1,0:T(8,128)} copy(f32[128,64,128]{2,0,1:T(8,128)} %get-tuple-element.23) | data formatting | bytes 8388608
  260.1 5.5 %fusion.24 = f32[96,64,128]{2,1,0:T(8,128)} fusion(f32[96,64,128]{2,1,0:T(8,128)S(1)} %copy-done.4, bf16[96,64,128]{2,1,0:T(8,128)(2,1)} %param.25, bf16[96,256,128]{2,1,0:T(8,128)(2,1)} %bitcast.86, bf16[96,64,320]{2,1,0:T(8,128)(2,1)S(1)} %bitcast.85, f32[96,64]{1,0:T(8,128)S(1)} %bitcast.88, f32[96,64]{1,0:T(8,128)S(1)} %copy.31, ...), kind=kOutput, calls=%fused_computation.44 | convolution fusion | flops 408158208 | bytes 17400320 | tf_op jit(solution)/shard_map/roj,rjs->ros/dot_general | solution.py:23
  266.4 4.9 %fusion.12 = f32[128,64,128]{2,1,0:T(8,128)} fusion(f32[128,64,128]{2,1,0:T(8,128)S(1)} %copy-done.2, bf16[128,64,128]{2,1,0:T(8,128)(2,1)S(1)} %copy-done, bf16[128,64,128]{2,1,0:T(8,128)(2,1)} %collective-permute-done.3, bf16[128,64,128]{2,1,0:T(8,128)(2,1)S(1)} %copy-done.8, f32[]{:T(128)S(6)} %convert_element_type.65), kind=kOutput, calls=%fused_computation.23 | convolution fusion | flops 279969792 | bytes 14680068 | tf_op jit(solution)/shard_map/roj,rjs->ros/dot_general | solution.py:23
  (83 shorter events, 19.6 us)
Async XLA Ops:
  0.6 1.6 copy-start
  2.2 13.0 %slice-start = ((s8[4718592]{0:T(1024)(128)(4,1)}), s8[4194304]{0:T(1024)(128)(4,1)S(1)}, s32[]{:S(2)}) async-start(s8[4718592]{0:T(1024)(128)(4,1)} %bitcast.80), calls=%async_computation | async-start | bytes 8388608
  5.9 9.3 %slice-start.1 = ((s8[4718592]{0:T(1024)(128)(4,1)}), s8[524288]{0:T(1024)(128)(4,1)S(1)}, s32[]{:S(2)}) async-start(s8[4718592]{0:T(1024)(128)(4,1)} %bitcast.80), calls=%async_computation.1 | async-start | bytes 1048576
  5.9 9.3 %copy-start.5 = (f32[96,64,128]{2,1,0:T(8,128)S(1)}, f32[96,64,128]{2,1,0:T(8,128)}, u32[]{:S(2)}) copy-start(f32[96,64,128]{2,1,0:T(8,128)} %param.28) | copy-start | bytes 9437188
  10.2 48.3 %collective-permute-start = (f32[128,64,128]{2,1,0:T(8,128)}, f32[128,64,128]{2,1,0:T(8,128)}, u32[]{:S(2)}, u32[]{:S(2)}) collective-permute-start(f32[128,64,128]{2,1,0:T(8,128)} %get-tuple-element.16), channel_id=1, source_target_pairs={{0,1},{1,2},{2,3},{3,4},{4,5},{5,6},{6,7},{8,9},{9,10},{10,11},{11... | collective-permute-start | bytes 12582920 | tf_op jit(solution)/shard_map/ppermute | solution.py:19
  22.1 12.8 %copy-start.14 = (s32[96,4]{0,1:T(4,128)S(1)}, s32[96,4]{0,1:T(4,128)}, u32[]{:S(2)}) copy-start(s32[96,4]{0,1:T(4,128)} %param.17) | copy-start | bytes 4612
  22.1 13.0 %copy-start.15 = (s32[128]{0:T(128)S(1)}, s32[128]{0:T(128)}, u32[]{:S(2)}) copy-start(s32[128]{0:T(128)} %param.19) | copy-start | bytes 1540
  22.1 13.1 %copy-start.16 = (s32[128]{0:T(128)S(1)}, s32[128]{0:T(128)}, u32[]{:S(2)}) copy-start(s32[128]{0:T(128)} %param.20) | copy-start | bytes 1540
  41.9 16.7 %copy-start.9 = (f32[128,64,128]{2,1,0:T(8,128)S(1)}, f32[128,64,128]{2,1,0:T(8,128)}, u32[]{:S(2)}) copy-start(f32[128,64,128]{2,1,0:T(8,128)} %param.27) | copy-start | bytes 12582916
  41.9 16.7 %copy-start.10 = (f32[128,64]{0,1:T(8,128)S(1)}, f32[128,64]{0,1:T(8,128)}, u32[]{:S(2)}) copy-start(f32[128,64]{0,1:T(8,128)} %param.23) | copy-start | bytes 98308
  78.5 8.2 %collective-permute-start.1 = (bf16[128,64,128]{2,1,0:T(8,128)(2,1)}, bf16[128,64,128]{2,1,0:T(8,128)(2,1)}, u32[]{:S(2)}, u32[]{:S(2)}) collective-permute-start(bf16[128,64,128]{2,1,0:T(8,128)(2,1)} %gather_fusion.3), channel_id=1, source_target_pairs={{1,0},{2,1},{3,2},{4,3},{5,4},{6,5},{7,6},{9,8},{10,9},{11,10},{12... | collective-permute-start | bytes 6291464 | tf_op jit(solution)/shard_map/ppermute | solution.py:19
  91.4 2.0 copy-start.1
  94.7 32.7 %copy-start.17 = (s32[96]{0:T(128)S(1)}, s32[96]{0:T(128)}, u32[]{:S(2)}) copy-start(s32[96]{0:T(128)} %param.18) | copy-start | bytes 1156
  94.7 52.2 %copy-start.11 = (f32[128,64]{0,1:T(8,128)S(1)}, f32[128,64]{0,1:T(8,128)}, u32[]{:S(2)}) copy-start(f32[128,64]{0,1:T(8,128)} %param.26) | copy-start | bytes 98308
  94.7 52.2 %copy-start.12 = (f32[128,64]{0,1:T(8,128)S(1)}, f32[128,64]{0,1:T(8,128)}, u32[]{:S(2)}) copy-start(f32[128,64]{0,1:T(8,128)} %param.22) | copy-start | bytes 98308
  94.7 52.5 %copy-start.13 = (f32[96,64]{0,1:T(8,128)S(1)}, f32[96,64]{0,1:T(8,128)}, u32[]{:S(2)}) copy-start(f32[96,64]{0,1:T(8,128)} %param.24) | copy-start | bytes 73732
  98.9 105.9 %collective-permute-start.2 = (f32[128,64,128]{2,1,0:T(8,128)}, f32[128,64,128]{2,1,0:T(8,128)}, u32[]{:S(2)}, u32[]{:S(2)}) collective-permute-start(f32[128,64,128]{2,1,0:T(8,128)} %get-tuple-element.14), channel_id=1, source_target_pairs={{0,1},{1,2},{2,3},{3,4},{4,5},{5,6},{6,7},{8,9},{9,10},{10,11},{11... | collective-permute-start | bytes 12582920 | tf_op jit(solution)/shard_map/ppermute | solution.py:19
  150.3 14.1 %slice-start.2 = ((s8[4718592]{0:T(1024)(128)(4,1)}), s8[524288]{0:T(1024)(128)(4,1)S(1)}, s32[]{:S(2)}) async-start(s8[4718592]{0:T(1024)(128)(4,1)} %bitcast.82), calls=%async_computation.2 | async-start | bytes 1048576
  156.0 8.4 %slice-start.3 = ((s8[4718592]{0:T(1024)(128)(4,1)}), s8[4194304]{0:T(1024)(128)(4,1)S(1)}, s32[]{:S(2)}) async-start(s8[4718592]{0:T(1024)(128)(4,1)} %bitcast.82), calls=%async_computation.3 | async-start | bytes 8388608
  162.8 1.7 copy-start.3
  183.5 16.6 %copy-start.7 = (f32[128,64,128]{2,1,0:T(8,128)S(1)}, f32[128,64,128]{2,1,0:T(8,128)}, u32[]{:S(2)}) copy-start(f32[128,64,128]{2,1,0:T(8,128)} %get-tuple-element.15) | copy-start | bytes 12582916
  200.1 4.7 %copy-start.6 = (f32[128,64,128]{2,0,1:T(8,128)S(1)}, f32[128,64,128]{2,0,1:T(8,128)}, u32[]{:S(2)}) copy-start(f32[128,64,128]{2,0,1:T(8,128)} %get-tuple-element.19) | copy-start | bytes 12582916
  221.1 44.5 %collective-permute-start.3 = (bf16[128,64,128]{2,1,0:T(8,128)(2,1)}, bf16[128,64,128]{2,1,0:T(8,128)(2,1)}, u32[]{:S(2)}, u32[]{:S(2)}) collective-permute-start(bf16[128,64,128]{2,1,0:T(8,128)(2,1)} %gather_fusion.7), channel_id=1, source_target_pairs={{1,0},{2,1},{3,2},{4,3},{5,4},{6,5},{7,6},{9,8},{10,9},{11,10},{12... | collective-permute-start | bytes 6291464 | tf_op jit(solution)/shard_map/ppermute | solution.py:19
  249.5 10.6 %slice-start.4 = ((s8[4718592]{0:T(1024)(128)(4,1)}), s8[524288]{0:T(1024)(128)(4,1)S(1)}, s32[]{:S(2)}) async-start(s8[4718592]{0:T(1024)(128)(4,1)} %bitcast.84), calls=%async_computation.4 | async-start | bytes 1048576
  253.3 6.8 %slice-start.5 = ((s8[4718592]{0:T(1024)(128)(4,1)}), s8[4194304]{0:T(1024)(128)(4,1)S(1)}, s32[]{:S(2)}) async-start(s8[4718592]{0:T(1024)(128)(4,1)} %bitcast.84), calls=%async_computation.5 | async-start | bytes 8388608
  253.3 6.8 %copy-start.4 = (f32[96,64,128]{2,1,0:T(8,128)S(1)}, f32[96,64,128]{2,1,0:T(8,128)}, u32[]{:S(2)}) copy-start(f32[96,64,128]{2,1,0:T(8,128)} %copy-done.3) | copy-start | bytes 9437188
  260.1 5.6 %copy-start.2 = (f32[128,64,128]{2,1,0:T(8,128)S(1)}, f32[128,64,128]{2,1,0:T(8,128)}, u32[]{:S(2)}) copy-start(f32[128,64,128]{2,1,0:T(8,128)} %copy-done.1) | copy-start | bytes 12582916
  260.1 6.3 %copy-start.8 = (bf16[128,64,128]{2,1,0:T(8,128)(2,1)S(1)}, bf16[128,64,128]{2,1,0:T(8,128)(2,1)}, u32[]{:S(2)}) copy-start(bf16[128,64,128]{2,1,0:T(8,128)(2,1)} %gather_fusion.6) | copy-start | bytes 6291460
where the time goes:
time: 276 us; the launch traced here: 272 us
  matrix products  117 us (42%)
  local copies, waits for them, and re-layouts  80.6 us (29%)
  blocking collectives  34.8 us (13%)
  starting transfers between devices  33.4 us (12%)
  other arithmetic  3.58 us (1%)
    dot_general x6, matrix products, sum_into(): jnp.einsum('bk,kos->bos', selector, terms, precision=lax.Precision.HIGHES...  67.9 us
    psum x2, blocking collectives, body(): lax.psum(grad_part.astype(jnp.bfloat16), 'scen').astype(jnp.float32)  34.8 us
    ppermute x4, starting transfers between devices, from_behind(): return lax.ppermute(value, axis, pairs)  33.4 us
    dot_general x2, local copies, waits for them, and re-layouts, transpose_blocks(): jnp.einsum('roj,ros->rjs', block_mats, dual_rows, preferred_element_type=...  25.5 us
    dot_general x4, matrix products, apply_blocks(): jnp.einsum('roj,rjs->ros', block_mats, stacked, preferred_element_type=jn...  21.9 us
    dot_general x4, matrix products, transpose_blocks(): jnp.einsum('roj,ros->rjs', block_mats, dual_rows, preferred_element_type=...  18.3 us
    unnamed x51, local copies, waits for them, and re-layouts  13 us
    gather x2, local copies, waits for them, and re-layouts, body(): gathered = second_bar[w_pattern].reshape(row_count, lead, scen_dev)  11.3 us
  transfers between devices with their start and end apart: 4, of which 1 were waited for; matrix products, arithmetic and copies ran while one was open for 50% of the time, Pallas kernels for 0%

commit v1 on v0

--- a/solution.py
+++ b/solution.py
@@ -98,7 +98,9 @@
         left_terms = from_behind(tie_terms[:, BLK:], "net", 1)
         grad_second = grad_second + sum_into(right_select, own_terms)
         grad_second = grad_second + sum_into(left_select, left_terms)
-        grad_first = lax.psum(grad_part.astype(jnp.bfloat16), "scen").astype(jnp.float32)
+        grad_first = jnp.sum(lax.all_gather(grad_part.astype(jnp.bfloat16), "scen"), axis=0).astype(
+            jnp.float32
+        )
         first_next = jnp.clip(first_now - first_step * (commit_cost - grad_first), 0.0, 1.0)
         second_next = jnp.maximum(second_now - primal_step * (cost_col - grad_second), 0.0)
         first_bar = (2.0 * first_next - first_now).astype(jnp.bfloat16)

time: 276 us -> 266 us (0.964)
  blocking collectives: 34.8 us -> 24.9 us
    psum x2 -> x0, blocking collectives: 34.8 us -> none  [body(): lax.psum(grad_part.astype(jnp.bfloat16), 'scen').astype(jnp.float32)]
    all_gather x0 -> x2, blocking collectives: none -> 24.9 us  [body(): lax.all_gather(grad_part.astype(jnp.bfloat16), 'scen')]
  transfers between devices with their start and end apart: 4 -> 4, of which waited for: 1 -> 1; matrix products, arithmetic and copies ran while one was open for 50% -> 52% of each run, Pallas kernels for 0% -> 0%
where the time goes in v1:
time: 266 us; the launch traced here: 262 us
  matrix products  117 us (44%)
  local copies, waits for them, and re-layouts  80.6 us (30%)
  starting transfers between devices  33.4 us (13%)
  blocking collectives  24.9 us (9%)
  other arithmetic  3.76 us (1%)
    dot_general x6, matrix products, sum_into(): jnp.einsum('bk,kos->bos', selector, terms, precision=lax.Precision.HIGHES...  67.6 us
    ppermute x4, starting transfers between devices, from_behind(): return lax.ppermute(value, axis, pairs)  33.4 us
    dot_general x2, local copies, waits for them, and re-layouts, transpose_blocks(): jnp.einsum('roj,ros->rjs', block_mats, dual_rows, preferred_element_type=...  25.5 us
    all_gather x2, blocking collectives, body(): lax.all_gather(grad_part.astype(jnp.bfloat16), 'scen')  24.9 us
    dot_general x4, matrix products, apply_blocks(): jnp.einsum('roj,rjs->ros', block_mats, stacked, preferred_element_type=jn...  21.9 us
    dot_general x4, matrix products, transpose_blocks(): jnp.einsum('roj,ros->rjs', block_mats, dual_rows, preferred_element_type=...  18.3 us
    unnamed x51, local copies, waits for them, and re-layouts  13 us
    gather x2, local copies, waits for them, and re-layouts, body(): gathered = second_bar[w_pattern].reshape(row_count, lead, scen_dev)  11.3 us
  transfers between devices with their start and end apart: 4, of which 1 were waited for; matrix products, arithmetic and copies ran while one was open for 52% of the time, Pallas kernels for 0%

profile of v1, /device:TPU:0, one launch (start us, length us, event | category | flops | bytes accessed | tf_op | source)
XLA Modules:
  0.0 261.7 jit_solution(14452418326508924166)
XLA Ops:
  2.2 3.7 %convolution_bitcast_fusion.3 = f32[128,128,128]{2,1,0:T(8,128)S(1)} fusion(bf16[128,64,128]{2,1,0:T(8,128)(2,1)S(1)} %copy-done, f32[128,64,128]{2,1,0:T(8,128)} %param.29, f32[]{:T(128)S(6)} %convert_element_type.69), kind=kOutput, calls=%fused_computation.40 | convolution fusion | flops 270532608 | bytes 14680068 | tf_op jit(solution)/shard_map/roj,ros->rjs/dot_general | solution.py:27
  5.9 4.3 %fusion.85 = (f32[128,64,128]{2,1,0:T(8,128)}, f32[128,64,128]{2,1,0:T(8,128)}) fusion(f32[128,128,128]{2,1,0:T(8,128)S(1)} %convolution_bitcast_fusion.3), kind=kLoop, calls=%fused_computation.111 | loop fusion | bytes 16777216 | tf_op jit(solution)/shard_map/slice | solution.py:98
  10.2 4.3 %collective-permute-start = (f32[128,64,128]{2,1,0:T(8,128)}, f32[128,64,128]{2,1,0:T(8,128)}, u32[]{:S(2)}, u32[]{:S(2)}) collective-permute-start(f32[128,64,128]{2,1,0:T(8,128)} %get-tuple-element.24), channel_id=1, source_target_pairs={{0,1},{1,2},{2,3},{3,4},{4,5},{5,6},{6,7},{8,9},{9,10},{10,11},{11... | collective-permute-start | bytes 12582920 | tf_op jit(solution)/shard_map/ppermute | solution.py:19
  15.2 6.9 %convolution_bitcast_fusion.1 = f32[96,256,128]{1,2,0:T(8,128)} fusion(bf16[96,64,320]{2,1,0:T(8,128)(2,1)S(1)} %bitcast.85, f32[96,64,128]{2,1,0:T(8,128)S(1)} %copy-done.5, f32[96]{0:T(128)S(1)} %compare_convert_fusion), kind=kOutput, calls=%fused_computation.13 | convolution fusion | flops 404226048 | bytes 18874880 | tf_op jit(solution)/shard_map/roj,ros->rjs/dot_general | solution.py:27
  22.1 12.8 %copy.88 = f32[96,256,128]{2,1,0:T(8,128)} copy(f32[96,256,128]{1,2,0:T(8,128)} %convolution_bitcast_fusion.1) | data formatting | bytes 25165824 | tf_op jit(solution)/shard_map/roj,ros->rjs/dot_general | solution.py:27
  35.2 6.7 %fusion.20 = f32[128,64,128]{2,0,1:T(8,128)S(1)} fusion(f32[128,64,128]{2,1,0:T(8,128)} %get-tuple-element.25, s32[128]{0:T(128)S(1)} %copy-done.16), kind=kOutput, calls=%fused_computation.32 | convolution fusion | flops 1610629120 | bytes 8389120 | tf_op jit(solution)/shard_map/bk,kos->bos/dot_general | solution.py:35
  41.9 16.6 %fusion.2 = f32[128,64,128]{2,0,1:T(8,128)S(1)} fusion(f32[384,64,128]{2,1,0:T(8,128)} %bitcast.82, s32[384]{0:T(512)S(1)} %eq.57), kind=kOutput, calls=%fused_computation.10 | convolution fusion | flops 4831887360 | bytes 16778752 | tf_op jit(solution)/shard_map/bk,kos->bos/dot_general | solution.py:35
  58.6 13.3 %subtract_convert_fusion.1 = (bf16[128,64,128]{2,0,1:T(8,128)(2,1)S(1)}, f32[128,64,128]{2,0,1:T(8,128)}) fusion(f32[128,64,128]{2,1,0:T(8,128)S(1)} %copy-done.9, f32[128,64,128]{2,1,0:T(8,128)} %collective-permute-done, s32[128]{0:T(128)S(1)} %copy-done.15, f32[128,64,128]{2,0,1:T(8,128)S(1)} %fusion.2, f32[128,64,128]{2,0,1:T(8,128)S(1)} %fusion.20, ...), kind=kOutput, calls=%fused_computation.36 | convolution fusion | flops 1620066304 | bytes 23101952 | tf_op jit(solution)/shard_map/bk,kos->bos/dot_general | solution.py:35
  71.9 2.7 %copy.95 = bf16[128,64,128]{2,1,0:T(8,128)(2,1)} copy(bf16[128,64,128]{2,0,1:T(8,128)(2,1)S(1)} %get-tuple-element.26) | data formatting | bytes 4194304 | tf_op jit(solution)/shard_map/convert_element_type | solution.py:107
  74.5 3.7 %gather_fusion.3 = bf16[128,64,128]{2,1,0:T(8,128)(2,1)} fusion(bf16[128,64,128]{2,1,0:T(8,128)(2,1)} %copy.95, s32[1024]{0:T(1024)S(1)} %pad_clamp_fusion), kind=kCustom, calls=%fused_computation.3 | custom fusion | bytes 4194816 | tf_op jit(solution)/shard_map/gather | solution.py:108
  79.6 2.9 %convert_reduce_fusion.1 = f32[96,64]{1,0:T(8,128)S(1)} fusion(f32[96,64,128]{2,1,0:T(8,128)} %param.28, f32[96]{0:T(128)S(1)} %compare_convert_fusion), kind=kLoop, calls=%fused_computation.51 | loop fusion | flops 3139584 | bytes 3170688 | tf_op jit(solution)/shard_map/roj,ros->rj/reduce_sum | solution.py:87
  82.5 3.7 %gather_fusion.2 = bf16[128,64,128]{2,1,0:T(8,128)(2,1)} fusion(bf16[128,64,128]{2,1,0:T(8,128)(2,1)} %copy.95, s32[1024]{0:T(1024)S(1)} %pad_clamp_fusion.1), kind=kCustom, calls=%fused_computation.2 | custom fusion | bytes 4194816 | tf_op jit(solution)/shard_map/gather | solution.py:109
  86.5 4.7 %fusion.13 = f32[128,64,128]{2,1,0:T(8,128)S(1)} fusion(f32[128,64,128]{2,1,0:T(8,128)} %param.29, bf16[128,64,128]{2,1,0:T(8,128)(2,1)S(1)} %copy-done, bf16[128,64,128]{2,1,0:T(8,128)(2,1)} %collective-permute-done.1, bf16[128,64,128]{2,1,0:T(8,128)(2,1)} %gather_fusion.2, f32[]{:T(128)S(6)} %convert_element_type.69), kind=kOutput, calls=%fused_computation.25 | convolution fusion | flops 281018368 | bytes 14680068 | tf_op jit(solution)/shard_map/roj,rjs->ros/dot_general | solution.py:23
  94.5 4.2 %fusion.84 = (f32[128,64,128]{2,1,0:T(8,128)}, f32[128,64,128]{2,1,0:T(8,128)}) fusion(f32[128,128,128]{2,1,0:T(8,128)S(1)} %convolution_bitcast_fusion.2), kind=kLoop, calls=%fused_computation.110 | loop fusion | bytes 16777216 | tf_op jit(solution)/shard_map/slice | solution.py:98
  98.7 26.5 %collective-permute-start.2 = (f32[128,64,128]{2,1,0:T(8,128)}, f32[128,64,128]{2,1,0:T(8,128)}, u32[]{:S(2)}, u32[]{:S(2)}) collective-permute-start(f32[128,64,128]{2,1,0:T(8,128)} %get-tuple-element.22), channel_id=1, source_target_pairs={{0,1},{1,2},{2,3},{3,4},{4,5},{5,6},{6,7},{8,9},{9,10},{10,11},{11... | collective-permute-start | bytes 12582920 | tf_op jit(solution)/shard_map/ppermute | solution.py:19
  127.4 12.7 %all-gather = bf16[512,64]{0,1:T(8,128)(2,1)S(1)} all-gather(bf16[128,64]{0,1:T(8,128)(2,1)S(1)} %convolution_convert_fusion.1), channel_id=2, replica_groups=mesh['scen'=4,'net'=8] {'scen'}, dimensions={0}, use_global_device_ids=true | all-gather | bytes 81920 | tf_op jit(solution)/shard_map/all_gather | solution.py:101
  141.4 2.3 fusion.52
  143.7 5.7 %gather_fusion = bf16[384,64,128]{2,1,0:T(8,128)(2,1)} fusion(bf16[128,64,128]{2,1,0:T(8,128)(2,1)} %copy.95, s32[1024]{0:T(1024)S(1)} %pad_clamp_fusion.3), kind=kCustom, calls=%fused_computation | custom fusion | bytes 12584448 | tf_op jit(solution)/shard_map/gather | solution.py:111
  149.4 6.8 %convert_reduce_fusion = (f32[96,64]{1,0:T(8,128)S(1)}, f32[96,64,128]{2,1,0:T(8,128)S(1)}) fusion(f32[96,64]{1,0:T(8,128)S(1)} %bitcast.97, bf16[96,256,128]{2,1,0:T(8,128)(2,1)} %bitcast.91, bf16[96,64,320]{2,1,0:T(8,128)(2,1)} %param.15, bf16[96,64,128]{2,1,0:T(8,128)(2,1)} %param.25, f32[96,64]{1,0:T(8,128)S(1)} %copy.86, f32[96,64,128]{2,1,0:T(8,128)} %param.28, ...), kind=kOutput, calls=%fused_computation.49 | convolution fusion | flops 411297792 | bytes 17375616 | tf_op jit(solution)/shard_map/roj,rjs->ros/dot_general | solution.py:23
  157.8 6.4 %convolution_bitcast_fusion = f32[96,256,128]{1,2,0:T(8,128)} fusion(bf16[96,64,320]{2,1,0:T(8,128)(2,1)S(1)} %bitcast.87, f32[96,64,128]{2,1,0:T(8,128)S(1)} %get-tuple-element.29), kind=kOutput, calls=%fused_computation.12 | convolution fusion | flops 403439616 | bytes 18874368 | tf_op jit(solution)/shard_map/roj,ros->rjs/dot_general | solution.py:27
  164.2 12.6 %copy.97 = f32[96,256,128]{2,1,0:T(8,128)} copy(f32[96,256,128]{1,2,0:T(8,128)} %convolution_bitcast_fusion) | data formatting | bytes 25165824 | tf_op jit(solution)/shard_map/roj,ros->rjs/dot_general | solution.py:27
  176.9 16.8 %fusion = f32[128,64,128]{2,0,1:T(8,128)S(1)} fusion(f32[384,64,128]{2,1,0:T(8,128)} %bitcast.83, s32[384]{0:T(512)S(1)} %eq.57), kind=kOutput, calls=%fused_computation.8 | convolution fusion | flops 4831887360 | bytes 16778752 | tf_op jit(solution)/shard_map/bk,kos->bos/dot_general | solution.py:35
  193.7 4.7 %fusion.16 = f32[128,64,128]{2,0,1:T(8,128)S(1)} fusion(f32[128,64,128]{2,1,0:T(8,128)S(1)} %copy-done.7, s32[128]{0:T(128)S(1)} %copy-done.16), kind=kOutput, calls=%fused_computation.28 | convolution fusion | flops 1610629120 | bytes 8389120 | tf_op jit(solution)/shard_map/bk,kos->bos/dot_general | solution.py:35
  198.4 9.6 %subtract_convert_fusion = (bf16[128,64,128]{2,0,1:T(8,128)(2,1)S(1)}, f32[128,64,128]{2,0,1:T(8,128)}) fusion(f32[128,64,128]{2,0,1:T(8,128)S(1)} %copy-done.6, f32[128,64,128]{2,1,0:T(8,128)} %collective-permute-done.2, s32[128]{0:T(128)S(1)} %copy-done.15, f32[128,64,128]{2,0,1:T(8,128)S(1)} %fusion, f32[128,64,128]{2,0,1:T(8,128)S(1)} %fusion.16, ...), kind=kOutput, calls=%fused_computation.34 | convolution fusion | flops 1620066304 | bytes 23101952 | tf_op jit(solution)/shard_map/bk,kos->bos/dot_general | solution.py:35
  208.0 2.7 %copy.103 = bf16[128,64,128]{2,1,0:T(8,128)(2,1)} copy(bf16[128,64,128]{2,0,1:T(8,128)(2,1)S(1)} %get-tuple-element.30) | data formatting | bytes 4194304 | tf_op jit(solution)/shard_map/convert_element_type | solution.py:107
  210.6 3.8 %gather_fusion.7 = bf16[128,64,128]{2,1,0:T(8,128)(2,1)} fusion(bf16[128,64,128]{2,1,0:T(8,128)(2,1)} %copy.103, s32[1024]{0:T(1024)S(1)} %pad_clamp_fusion), kind=kCustom, calls=%fused_computation.7 | custom fusion | bytes 4194816 | tf_op jit(solution)/shard_map/gather | solution.py:108
  217.9 12.2 %all-gather.1 = bf16[512,64]{0,1:T(8,128)(2,1)S(1)} all-gather(bf16[128,64]{0,1:T(8,128)(2,1)S(1)} %convolution_convert_fusion), channel_id=3, replica_groups=mesh['scen'=4,'net'=8] {'scen'}, dimensions={0}, use_global_device_ids=true | all-gather | bytes 81920 | tf_op jit(solution)/shard_map/all_gather | solution.py:101
  234.0 5.6 %gather_fusion.4 = bf16[384,64,128]{2,1,0:T(8,128)(2,1)} fusion(bf16[128,64,128]{2,1,0:T(8,128)(2,1)} %copy.103, s32[1024]{0:T(1024)S(1)} %pad_clamp_fusion.3), kind=kCustom, calls=%fused_computation.4 | custom fusion | bytes 12584448 | tf_op jit(solution)/shard_map/gather | solution.py:111
  239.6 3.8 %gather_fusion.6 = bf16[128,64,128]{2,1,0:T(8,128)(2,1)} fusion(bf16[128,64,128]{2,1,0:T(8,128)(2,1)} %copy.103, s32[1024]{0:T(1024)S(1)} %pad_clamp_fusion.1), kind=kCustom, calls=%fused_computation.6 | custom fusion | bytes 4194816 | tf_op jit(solution)/shard_map/gather | solution.py:109
  243.4 6.8 %copy.107 = f32[128,64,128]{2,1,0:T(8,128)} copy(f32[128,64,128]{2,0,1:T(8,128)} %get-tuple-element.31) | data formatting | bytes 8388608
  250.3 5.5 %fusion.24 = f32[96,64,128]{2,1,0:T(8,128)} fusion(f32[96,64,128]{2,1,0:T(8,128)S(1)} %copy-done.4, bf16[96,64,128]{2,1,0:T(8,128)(2,1)} %param.25, bf16[96,256,128]{2,1,0:T(8,128)(2,1)} %bitcast.90, bf16[96,64,320]{2,1,0:T(8,128)(2,1)S(1)} %bitcast.89, f32[96,64]{1,0:T(8,128)S(1)} %bitcast.92, f32[96,64]{1,0:T(8,128)S(1)} %copy.86, ...), kind=kOutput, calls=%fused_computation.44 | convolution fusion | flops 408158208 | bytes 17400320 | tf_op jit(solution)/shard_map/roj,rjs->ros/dot_general | solution.py:23
  256.5 4.9 %fusion.12 = f32[128,64,128]{2,1,0:T(8,128)} fusion(f32[128,64,128]{2,1,0:T(8,128)S(1)} %copy-done.2, bf16[128,64,128]{2,1,0:T(8,128)(2,1)S(1)} %copy-done, bf16[128,64,128]{2,1,0:T(8,128)(2,1)} %collective-permute-done.3, bf16[128,64,128]{2,1,0:T(8,128)(2,1)S(1)} %copy-done.8, f32[]{:T(128)S(6)} %convert_element_type.69), kind=kOutput, calls=%fused_computation.23 | convolution fusion | flops 279969792 | bytes 14680068 | tf_op jit(solution)/shard_map/roj,rjs->ros/dot_general | solution.py:23
  (87 shorter events, 19.9 us)
Async XLA Ops:
  0.6 1.6 copy-start
  2.2 13.0 %slice-start = ((s8[4718592]{0:T(1024)(128)(4,1)}), s8[4194304]{0:T(1024)(128)(4,1)S(1)}, s32[]{:S(2)}) async-start(s8[4718592]{0:T(1024)(128)(4,1)} %bitcast.84), calls=%async_computation | async-start | bytes 8388608
  5.9 9.3 %slice-start.1 = ((s8[4718592]{0:T(1024)(128)(4,1)}), s8[524288]{0:T(1024)(128)(4,1)S(1)}, s32[]{:S(2)}) async-start(s8[4718592]{0:T(1024)(128)(4,1)} %bitcast.84), calls=%async_computation.1 | async-start | bytes 1048576
  5.9 9.3 %copy-start.5 = (f32[96,64,128]{2,1,0:T(8,128)S(1)}, f32[96,64,128]{2,1,0:T(8,128)}, u32[]{:S(2)}) copy-start(f32[96,64,128]{2,1,0:T(8,128)} %param.28) | copy-start | bytes 9437188
  10.2 48.3 %collective-permute-start = (f32[128,64,128]{2,1,0:T(8,128)}, f32[128,64,128]{2,1,0:T(8,128)}, u32[]{:S(2)}, u32[]{:S(2)}) collective-permute-start(f32[128,64,128]{2,1,0:T(8,128)} %get-tuple-element.24), channel_id=1, source_target_pairs={{0,1},{1,2},{2,3},{3,4},{4,5},{5,6},{6,7},{8,9},{9,10},{10,11},{11... | collective-permute-start | bytes 12582920 | tf_op jit(solution)/shard_map/ppermute | solution.py:19
  22.1 12.8 %copy-start.14 = (s32[96,4]{0,1:T(4,128)S(1)}, s32[96,4]{0,1:T(4,128)}, u32[]{:S(2)}) copy-start(s32[96,4]{0,1:T(4,128)} %param.17) | copy-start | bytes 4612
  22.1 13.0 %copy-start.15 = (s32[128]{0:T(128)S(1)}, s32[128]{0:T(128)}, u32[]{:S(2)}) copy-start(s32[128]{0:T(128)} %param.19) | copy-start | bytes 1540
  22.1 13.1 %copy-start.16 = (s32[128]{0:T(128)S(1)}, s32[128]{0:T(128)}, u32[]{:S(2)}) copy-start(s32[128]{0:T(128)} %param.20) | copy-start | bytes 1540
  41.9 16.7 %copy-start.9 = (f32[128,64,128]{2,1,0:T(8,128)S(1)}, f32[128,64,128]{2,1,0:T(8,128)}, u32[]{:S(2)}) copy-start(f32[128,64,128]{2,1,0:T(8,128)} %param.27) | copy-start | bytes 12582916
  41.9 16.7 %copy-start.10 = (f32[128,64]{0,1:T(8,128)S(1)}, f32[128,64]{0,1:T(8,128)}, u32[]{:S(2)}) copy-start(f32[128,64]{0,1:T(8,128)} %param.23) | copy-start | bytes 98308
  78.3 8.2 %collective-permute-start.1 = (bf16[128,64,128]{2,1,0:T(8,128)(2,1)}, bf16[128,64,128]{2,1,0:T(8,128)(2,1)}, u32[]{:S(2)}, u32[]{:S(2)}) collective-permute-start(bf16[128,64,128]{2,1,0:T(8,128)(2,1)} %gather_fusion.3), channel_id=1, source_target_pairs={{1,0},{2,1},{3,2},{4,3},{5,4},{6,5},{7,6},{9,8},{10,9},{11,10},{12... | collective-permute-start | bytes 6291464 | tf_op jit(solution)/shard_map/ppermute | solution.py:19
  91.2 2.0 copy-start.1
  94.5 32.7 %copy-start.17 = (s32[96]{0:T(128)S(1)}, s32[96]{0:T(128)}, u32[]{:S(2)}) copy-start(s32[96]{0:T(128)} %param.18) | copy-start | bytes 1156
  94.5 45.7 %copy-start.11 = (f32[128,64]{0,1:T(8,128)S(1)}, f32[128,64]{0,1:T(8,128)}, u32[]{:S(2)}) copy-start(f32[128,64]{0,1:T(8,128)} %param.26) | copy-start | bytes 98308
  94.5 45.7 %copy-start.12 = (f32[128,64]{0,1:T(8,128)S(1)}, f32[128,64]{0,1:T(8,128)}, u32[]{:S(2)}) copy-start(f32[128,64]{0,1:T(8,128)} %param.22) | copy-start | bytes 98308
  94.5 46.1 %copy-start.13 = (f32[96,64]{0,1:T(8,128)S(1)}, f32[96,64]{0,1:T(8,128)}, u32[]{:S(2)}) copy-start(f32[96,64]{0,1:T(8,128)} %param.24) | copy-start | bytes 73732
  98.7 99.6 %collective-permute-start.2 = (f32[128,64,128]{2,1,0:T(8,128)}, f32[128,64,128]{2,1,0:T(8,128)}, u32[]{:S(2)}, u32[]{:S(2)}) collective-permute-start(f32[128,64,128]{2,1,0:T(8,128)} %get-tuple-element.22), channel_id=1, source_target_pairs={{0,1},{1,2},{2,3},{3,4},{4,5},{5,6},{6,7},{8,9},{9,10},{10,11},{11... | collective-permute-start | bytes 12582920 | tf_op jit(solution)/shard_map/ppermute | solution.py:19
  143.7 14.1 %slice-start.2 = ((s8[4718592]{0:T(1024)(128)(4,1)}), s8[524288]{0:T(1024)(128)(4,1)S(1)}, s32[]{:S(2)}) async-start(s8[4718592]{0:T(1024)(128)(4,1)} %bitcast.86), calls=%async_computation.2 | async-start | bytes 1048576
  149.4 8.4 %slice-start.3 = ((s8[4718592]{0:T(1024)(128)(4,1)}), s8[4194304]{0:T(1024)(128)(4,1)S(1)}, s32[]{:S(2)}) async-start(s8[4718592]{0:T(1024)(128)(4,1)} %bitcast.86), calls=%async_computation.3 | async-start | bytes 8388608
  156.1 1.7 copy-start.3
  176.9 16.8 %copy-start.7 = (f32[128,64,128]{2,1,0:T(8,128)S(1)}, f32[128,64,128]{2,1,0:T(8,128)}, u32[]{:S(2)}) copy-start(f32[128,64,128]{2,1,0:T(8,128)} %get-tuple-element.23) | copy-start | bytes 12582916
  193.7 4.7 %copy-start.6 = (f32[128,64,128]{2,0,1:T(8,128)S(1)}, f32[128,64,128]{2,0,1:T(8,128)}, u32[]{:S(2)}) copy-start(f32[128,64,128]{2,0,1:T(8,128)} %get-tuple-element.27) | copy-start | bytes 12582916
  214.4 41.4 %collective-permute-start.3 = (bf16[128,64,128]{2,1,0:T(8,128)(2,1)}, bf16[128,64,128]{2,1,0:T(8,128)(2,1)}, u32[]{:S(2)}, u32[]{:S(2)}) collective-permute-start(bf16[128,64,128]{2,1,0:T(8,128)(2,1)} %gather_fusion.7), channel_id=1, source_target_pairs={{1,0},{2,1},{3,2},{4,3},{5,4},{6,5},{7,6},{9,8},{10,9},{11,10},{12... | collective-permute-start | bytes 6291464 | tf_op jit(solution)/shard_map/ppermute | solution.py:19
  239.6 10.6 %slice-start.4 = ((s8[4718592]{0:T(1024)(128)(4,1)}), s8[524288]{0:T(1024)(128)(4,1)S(1)}, s32[]{:S(2)}) async-start(s8[4718592]{0:T(1024)(128)(4,1)} %bitcast.88), calls=%async_computation.4 | async-start | bytes 1048576
  243.4 6.8 %slice-start.5 = ((s8[4718592]{0:T(1024)(128)(4,1)}), s8[4194304]{0:T(1024)(128)(4,1)S(1)}, s32[]{:S(2)}) async-start(s8[4718592]{0:T(1024)(128)(4,1)} %bitcast.88), calls=%async_computation.5 | async-start | bytes 8388608
  243.4 6.8 %copy-start.4 = (f32[96,64,128]{2,1,0:T(8,128)S(1)}, f32[96,64,128]{2,1,0:T(8,128)}, u32[]{:S(2)}) copy-start(f32[96,64,128]{2,1,0:T(8,128)} %copy-done.3) | copy-start | bytes 9437188
  250.2 5.6 %copy-start.2 = (f32[128,64,128]{2,1,0:T(8,128)S(1)}, f32[128,64,128]{2,1,0:T(8,128)}, u32[]{:S(2)}) copy-start(f32[128,64,128]{2,1,0:T(8,128)} %copy-done.1) | copy-start | bytes 12582916
  250.2 6.3 %copy-start.8 = (bf16[128,64,128]{2,1,0:T(8,128)(2,1)S(1)}, bf16[128,64,128]{2,1,0:T(8,128)(2,1)}, u32[]{:S(2)}) copy-start(bf16[128,64,128]{2,1,0:T(8,128)(2,1)} %gather_fusion.6) | copy-start | bytes 6291460
